TPU v7x, 512 devices: a whole 4x4x16 slice. The times are simulated.
512 devices in a mesh: dp: 256 (over z, y_hi, x, core), sub: 2 (over y_lo).
Axes of the slice: x: 4, y: 4 (y_hi: 2, y_lo: 2; y = y_hi * 2 + y_lo), z: 16, core: 2. Of those that a mesh axis runs over, the one named last changes fastest.
Arguments:
- photo_vectors: bfloat16 [131072, 1024], P(('dp', 'sub')), may hold values from -40 to 40
- caption_vectors: bfloat16 [131072, 1024], P(('dp', 'sub')), may hold values from -40 to 40
- inverse_heat_factor: float32 [1], replicated, may hold values from 1 to 4
Outputs:
- picture_gradient: float32 [131072, 1024], P(('dp', 'sub'))
- text_grad: float32 [131072, 1024], P(('dp', 'sub'))
All inputs are finite; a program needn't handle non-finite values.
Results may differ from a plain program's by a relative error of at most 0.002.
Values may be sent and summed in bfloat16 or wider, within the bound.
A program may use at most 64 MiB of HBM per device.

v0:
```python
import math

import jax
import jax.numpy as jnp
from jax import lax
from jax.sharding import PartitionSpec as P

BAND = 4


def shifted(value, axis, steps):
    count = lax.axis_size(axis)
    pairs = [(source, (source + steps) % count) for source in range(count)]
    return lax.ppermute(value, axis, pairs)


def joined(part, axis, combine):
    gathered = lax.all_gather(part, axis)

    def take(source):
        return lax.dynamic_index_in_dim(gathered, source, 0, False)

    return lax.fori_loop(
        1, lax.axis_size(axis), lambda source, state: combine(state, take(source)), take(0)
    )


def inner(left, right):
    return lax.dot_general(
        left, right, (((1,), (1,)), ((), ())), preferred_element_type=jnp.float32
    )


def across(weight, rows):
    return lax.dot_general(
        weight, rows, (((0,), (0,)), ((), ())), preferred_element_type=jnp.float32
    )


def local(photo_vectors, caption_vectors, inverse_heat_factor):
    rows = photo_vectors.shape[0]
    diagonal_lane_extent = photo_vectors.shape[1]
    half = lax.axis_index("sub")
    similarity_multiplier = inverse_heat_factor[0] * (1.0 / math.sqrt(diagonal_lane_extent))
    block = lax.all_gather(caption_vectors, "sub", axis=0, tiled=True)
    total_rows = block.shape[0]
    kept = []
    row_fragments = []
    col_run = None
    for step in range(BAND):
        kept.append(block)
        logits = similarity_multiplier * inner(photo_vectors, block)
        row_fragments.append(jax.nn.logsumexp(logits, axis=1))
        piece = jax.nn.logsumexp(logits, axis=0)
        col_run = piece if step == 0 else jnp.logaddexp(col_run, piece)
        if step + 1 < BAND:
            block = shifted(block, "dp", -1)
            col_run = shifted(col_run, "dp", -1)
    col_lse = joined(col_run, "sub", jnp.logaddexp)
    row_lse = jax.nn.logsumexp(jnp.stack(row_fragments, 1), axis=1)
    lines = jnp.arange(rows) + half * rows
    diag_mask = (jnp.arange(total_rows)[None, :] == lines[:, None]).astype(jnp.float32)
    accum = jnp.zeros((total_rows, diagonal_lane_extent), jnp.float32)
    grad_img = jnp.zeros((rows, diagonal_lane_extent), jnp.float32)
    for step in range(BAND):
        ahead = BAND - 1 - step
        present_offset = block
        logits = similarity_multiplier * inner(photo_vectors, present_offset)
        weight = jnp.exp(logits - row_lse[:, None]) + jnp.exp(logits - col_lse[None, :])
        if ahead == 0:
            weight = weight - 2.0 * diag_mask
        weight = (0.5 * similarity_multiplier * weight).astype(jnp.bfloat16)
        grad_img = grad_img + jnp.dot(weight, present_offset, preferred_element_type=jnp.float32)
        accum = accum + across(weight, photo_vectors)
        if step + 1 < BAND:
            block = shifted(present_offset, "dp", 1)
            accum, col_lse = shifted((accum, col_lse), "dp", 1)
    grad_text = lax.psum_scatter(accum, "sub", scatter_dimension=0, tiled=True)
    return (grad_img, grad_text)


def solution(mesh):
    in_specs = (P(("dp", "sub"), None), P(("dp", "sub"), None), P())
    out_specs = (P(("dp", "sub"), None), P(("dp", "sub"), None))
    return jax.shard_map(local, mesh=mesh, in_specs=in_specs, out_specs=out_specs, check_vma=False)
```

profile of v0, /device:TPU:1, one launch (start us, length us, event | category | flops | bytes accessed | tf_op | source)
XLA Modules:
  0.0 304.2 jit_solution(6954919141063591459)
XLA Ops:
  7.2 0.7 all-gather.4.cloned.1.call-update
  8.6 38.4 %all-gather.4.cloned.1.call-done = bf16[512,1024]{1,0:T(8,128)(2,1)} async-done(((bf16[256,1024]{1,0:T(8,128)(2,1)}), bf16[512,1024]{1,0:T(8,128)(2,1)}) %all-gather.4.cloned.1.call-update) | async-done | bytes 1048592 | tf_op jit(solution)/shard_map/all_gather | solution.py:45
  47.0 2.6 collective-permute-start
  49.5 1.8 fusion.11
  51.6 9.7 %collective-permute-start.3 = (f32[512]{0:T(512)S(1)}, f32[512]{0:T(512)S(1)}, u32[]{:S(2)}, u32[]{:S(2)}) collective-permute-start(f32[512]{0:T(512)S(1)} %log_add_fusion.3), channel_id=1, source_target_pairs={{0,510},{2,0},{4,2},{6,4},{8,6},{10,8},{12,10},{14,12},{16,14},{18... | collective-permute-start | bytes 6152 | tf_op jit(solution)/shard_map/ppermute | solution.py:14
  61.3 2.0 collective-permute-done
  63.3 8.5 %collective-permute-start.1 = (bf16[512,1024]{1,0:T(8,128)(2,1)S(1)}, bf16[512,1024]{1,0:T(8,128)(2,1)S(1)}, u32[]{:S(2)}, u32[]{:S(2)}) collective-permute-start(bf16[512,1024]{1,0:T(8,128)(2,1)S(1)} %collective-permute-done), channel_id=1, source_target_pairs={{0,510},{2,0},{4,2},{6,4},{8,6},{10,8},{12,10},{14,12},{16,14},{18... | collective-permute-start | bytes 3145736 | tf_op jit(solution)/shard_map/ppermute | solution.py:14
  72.7 9.4 %collective-permute-start.4 = (f32[512]{0:T(512)S(1)}, f32[512]{0:T(512)S(1)}, u32[]{:S(2)}, u32[]{:S(2)}) collective-permute-start(f32[512]{0:T(512)S(1)} %add_select_fusion.2), channel_id=1, source_target_pairs={{0,510},{2,0},{4,2},{6,4},{8,6},{10,8},{12,10},{14,12},{16,14},{18... | collective-permute-start | bytes 6152 | tf_op jit(solution)/shard_map/ppermute | solution.py:14
  82.1 11.4 %collective-permute-start.2 = (bf16[512,1024]{1,0:T(8,128)(2,1)S(1)}, bf16[512,1024]{1,0:T(8,128)(2,1)S(1)}, u32[]{:S(2)}, u32[]{:S(2)}) collective-permute-start(bf16[512,1024]{1,0:T(8,128)(2,1)S(1)} %collective-permute-done.1), channel_id=1, source_target_pairs={{0,510},{2,0},{4,2},{6,4},{8,6},{10,8},{12,10},{14,12},{16,14},{18... | collective-permute-start | bytes 3145736 | tf_op jit(solution)/shard_map/ppermute | solution.py:14
  93.5 0.6 fusion.9
  94.4 9.5 %collective-permute-start.5 = (f32[512]{0:T(512)S(1)}, f32[512]{0:T(512)S(1)}, u32[]{:S(2)}, u32[]{:S(2)}) collective-permute-start(f32[512]{0:T(512)S(1)} %add_select_fusion.1), channel_id=1, source_target_pairs={{0,510},{2,0},{4,2},{6,4},{8,6},{10,8},{12,10},{14,12},{16,14},{18... | collective-permute-start | bytes 6152 | tf_op jit(solution)/shard_map/ppermute | solution.py:14
  104.9 3.2 %all-gather.1 = f32[2,1,512]{2,1,0:T(1,128)S(1)} all-gather(f32[1,1,512]{2,1,0:T(1,128)S(1)} %bitcast.58), channel_id=2, replica_groups=mesh['dp'=256,'sub'=2] {'sub'}, dimensions={0}, use_global_device_ids=true | all-gather | bytes 6144 | tf_op jit(solution)/shard_map/all_gather | solution.py:18
  108.8 1.9 collective-permute-start.12
  110.7 1.9 collective-permute-start.6
  112.7 1.9 collective-permute-start.7
  114.6 30.3 %collective-permute-done.7 = f32[512]{0:T(512)S(1)} collective-permute-done((f32[512]{0:T(512)S(1)}, f32[512]{0:T(512)S(1)}, u32[]{:S(2)}, u32[]{:S(2)}) %collective-permute-start.7) | collective-permute-done | bytes 2080 | tf_op jit(solution)/shard_map/ppermute | solution.py:14
  146.0 4.4 %collective-permute-start.13 = (f32[512,1024]{1,0:T(8,128)S(1)}, f32[512,1024]{1,0:T(8,128)S(1)}, u32[]{:S(2)}, u32[]{:S(2)}) collective-permute-start(f32[512,1024]{1,0:T(8,128)S(1)} %convolution_add_fusion), channel_id=1, source_target_pairs={{0,2},{2,4},{4,6},{6,8},{8,10},{10,12},{12,14},{14,16},{16,18},{18... | collective-permute-start | bytes 6291464 | tf_op jit(solution)/shard_map/ppermute | solution.py:14
  150.4 1.9 collective-permute-start.8
  152.3 1.9 collective-permute-start.9
  154.3 30.3 %collective-permute-done.9 = f32[512]{0:T(512)S(1)} collective-permute-done((f32[512]{0:T(512)S(1)}, f32[512]{0:T(512)S(1)}, u32[]{:S(2)}, u32[]{:S(2)}) %collective-permute-start.9) | collective-permute-done | bytes 2080 | tf_op jit(solution)/shard_map/ppermute | solution.py:14
  184.6 1.8 multiply_convert_fusion.1
  187.5 4.5 %collective-permute-start.14 = (f32[512,1024]{1,0:T(8,128)S(1)}, f32[512,1024]{1,0:T(8,128)}, u32[]{:S(2)}, u32[]{:S(2)}) collective-permute-start(f32[512,1024]{1,0:T(8,128)S(1)} %add.199), channel_id=1, source_target_pairs={{0,2},{2,4},{4,6},{6,8},{8,10},{10,12},{12,14},{14,16},{16,18},{18... | collective-permute-start | bytes 6291464 | tf_op jit(solution)/shard_map/ppermute | solution.py:14
  192.0 1.9 collective-permute-start.10
  193.9 1.9 collective-permute-start.11
  195.9 30.4 %collective-permute-done.11 = f32[512]{0:T(512)S(1)} collective-permute-done((f32[512]{0:T(512)S(1)}, f32[512]{0:T(512)S(1)}, u32[]{:S(2)}, u32[]{:S(2)}) %collective-permute-start.11) | collective-permute-done | bytes 2080 | tf_op jit(solution)/shard_map/ppermute | solution.py:14
  226.3 1.8 multiply_convert_fusion
  228.2 0.7 copy-done.7
  229.3 3.3 %add.200 = f32[512,1024]{1,0:T(8,128)} add(f32[512,1024]{1,0:T(8,128)} %collective-permute-done.14, f32[512,1024]{1,0:T(8,128)S(1)} %fusion.13) | non-fusion elementwise | flops 524288 | bytes 6291456 | tf_op jit(solution)/shard_map/add | solution.py:74
  232.7 1.2 copy-done.2
  235.4 1.7 convolution_add_fusion.2
  237.1 2.6 convolution_add_fusion.1
  239.7 57.6 %reduce-scatter.2.cloned.1.call-done = f32[256,1024]{1,0:T(8,128)} async-done(((f32[512,1024]{1,0:T(8,128)}), f32[256,1024]{1,0:T(8,128)}) %reduce-scatter.2.cloned.1.call-update) | async-done | bytes 1048592 | tf_op jit(solution)/shard_map/reduce_scatter | solution.py:78
  (65 shorter events, 7.1 us)
Async XLA Ops:
  7.2 42.4 %copy-start = (bf16[256,1024]{1,0:T(8,128)(2,1)S(1)}, bf16[256,1024]{1,0:T(8,128)(2,1)}, u32[]{:S(2)}) copy-start(bf16[256,1024]{1,0:T(8,128)(2,1)} %param.3) | copy-start | bytes 1572868
  7.2 39.8 %all-gather.4.cloned.1.call-start = ((), (), s32[]{:S(2)}) async-start(), calls=%async_computation.1 | async-start | bytes 1572864 | tf_op jit(solution)/shard_map/all_gather | solution.py:45
  7.9 289.4 %reduce-scatter.2.cloned.1.call-start = ((), (), s32[]{:S(2)}) async-start(), calls=%async_computation.2 | async-start | bytes 3145728 | tf_op jit(solution)/shard_map/reduce_scatter | solution.py:78
  47.0 16.3 %collective-permute-start = (bf16[512,1024]{1,0:T(8,128)(2,1)}, bf16[512,1024]{1,0:T(8,128)(2,1)S(1)}, u32[]{:S(2)}, u32[]{:S(2)}) collective-permute-start(bf16[512,1024]{1,0:T(8,128)(2,1)} %all-gather.4.cloned.1.call-done), channel_id=1, source_target_pairs={{0,510},{2,0},{4,2},{6,4},{8,6},{10,8},{12,10},{14,12},{16,14},{18... | collective-permute-start | bytes 3145736 | tf_op jit(solution)/shard_map/ppermute | solution.py:14
  51.6 21.1 %collective-permute-start.3 = (f32[512]{0:T(512)S(1)}, f32[512]{0:T(512)S(1)}, u32[]{:S(2)}, u32[]{:S(2)}) collective-permute-start(f32[512]{0:T(512)S(1)} %log_add_fusion.3), channel_id=1, source_target_pairs={{0,510},{2,0},{4,2},{6,4},{8,6},{10,8},{12,10},{14,12},{16,14},{18... | collective-permute-start | bytes 6152 | tf_op jit(solution)/shard_map/ppermute | solution.py:14
  63.3 18.8 %collective-permute-start.1 = (bf16[512,1024]{1,0:T(8,128)(2,1)S(1)}, bf16[512,1024]{1,0:T(8,128)(2,1)S(1)}, u32[]{:S(2)}, u32[]{:S(2)}) collective-permute-start(bf16[512,1024]{1,0:T(8,128)(2,1)S(1)} %collective-permute-done), channel_id=1, source_target_pairs={{0,510},{2,0},{4,2},{6,4},{8,6},{10,8},{12,10},{14,12},{16,14},{18... | collective-permute-start | bytes 3145736 | tf_op jit(solution)/shard_map/ppermute | solution.py:14
  72.7 21.7 %collective-permute-start.4 = (f32[512]{0:T(512)S(1)}, f32[512]{0:T(512)S(1)}, u32[]{:S(2)}, u32[]{:S(2)}) collective-permute-start(f32[512]{0:T(512)S(1)} %add_select_fusion.2), channel_id=1, source_target_pairs={{0,510},{2,0},{4,2},{6,4},{8,6},{10,8},{12,10},{14,12},{16,14},{18... | collective-permute-start | bytes 6152 | tf_op jit(solution)/shard_map/ppermute | solution.py:14
  82.1 21.9 %collective-permute-start.2 = (bf16[512,1024]{1,0:T(8,128)(2,1)S(1)}, bf16[512,1024]{1,0:T(8,128)(2,1)S(1)}, u32[]{:S(2)}, u32[]{:S(2)}) collective-permute-start(bf16[512,1024]{1,0:T(8,128)(2,1)S(1)} %collective-permute-done.1), channel_id=1, source_target_pairs={{0,510},{2,0},{4,2},{6,4},{8,6},{10,8},{12,10},{14,12},{16,14},{18... | collective-permute-start | bytes 3145736 | tf_op jit(solution)/shard_map/ppermute | solution.py:14
  94.4 10.4 %collective-permute-start.5 = (f32[512]{0:T(512)S(1)}, f32[512]{0:T(512)S(1)}, u32[]{:S(2)}, u32[]{:S(2)}) collective-permute-start(f32[512]{0:T(512)S(1)} %add_select_fusion.1), channel_id=1, source_target_pairs={{0,510},{2,0},{4,2},{6,4},{8,6},{10,8},{12,10},{14,12},{16,14},{18... | collective-permute-start | bytes 6152 | tf_op jit(solution)/shard_map/ppermute | solution.py:14
  104.0 6.7 %copy-start.1 = (bf16[512,1024]{1,0:T(8,128)(2,1)}, bf16[512,1024]{1,0:T(8,128)(2,1)S(1)}, u32[]{:S(2)}) copy-start(bf16[512,1024]{1,0:T(8,128)(2,1)S(1)} %collective-permute-done.2) | copy-start | bytes 3145732
  108.8 36.7 %collective-permute-start.12 = (f32[512,1024]{1,0:T(8,128)S(1)}, f32[512,1024]{1,0:T(8,128)S(1)}, u32[]{:S(2)}, u32[]{:S(2)}) collective-permute-start(f32[512,1024]{1,0:T(8,128)S(1)} %fusion.6), channel_id=1, source_target_pairs={{0,2},{2,4},{4,6},{6,8},{8,10},{10,12},{12,14},{14,16},{16,18},{18... | collective-permute-start | bytes 6291464 | tf_op jit(solution)/shard_map/ppermute | solution.py:14
  110.7 34.2 %collective-permute-start.6 = (bf16[512,1024]{1,0:T(8,128)(2,1)S(1)}, bf16[512,1024]{1,0:T(8,128)(2,1)S(1)}, u32[]{:S(2)}, u32[]{:S(2)}) collective-permute-start(bf16[512,1024]{1,0:T(8,128)(2,1)S(1)} %collective-permute-done.2), channel_id=1, source_target_pairs={{0,2},{2,4},{4,6},{6,8},{8,10},{10,12},{12,14},{14,16},{16,18},{18... | collective-permute-start | bytes 3145736 | tf_op jit(solution)/shard_map/ppermute | solution.py:14
  112.7 32.3 %collective-permute-start.7 = (f32[512]{0:T(512)S(1)}, f32[512]{0:T(512)S(1)}, u32[]{:S(2)}, u32[]{:S(2)}) collective-permute-start(f32[512]{0:T(512)S(1)} %bitcast.51), channel_id=1, source_target_pairs={{0,2},{2,4},{4,6},{6,8},{8,10},{10,12},{12,14},{14,16},{16,18},{18... | collective-permute-start | bytes 6152 | tf_op jit(solution)/shard_map/ppermute | solution.py:14
  144.9 5.5 %copy-start.3 = (bf16[512,1024]{1,0:T(8,128)(2,1)}, bf16[512,1024]{1,0:T(8,128)(2,1)S(1)}, u32[]{:S(2)}) copy-start(bf16[512,1024]{1,0:T(8,128)(2,1)S(1)} %collective-permute-done.6) | copy-start | bytes 3145732
  146.0 41.1 %collective-permute-start.13 = (f32[512,1024]{1,0:T(8,128)S(1)}, f32[512,1024]{1,0:T(8,128)S(1)}, u32[]{:S(2)}, u32[]{:S(2)}) collective-permute-start(f32[512,1024]{1,0:T(8,128)S(1)} %convolution_add_fusion), channel_id=1, source_target_pairs={{0,2},{2,4},{4,6},{6,8},{8,10},{10,12},{12,14},{14,16},{16,18},{18... | collective-permute-start | bytes 6291464 | tf_op jit(solution)/shard_map/ppermute | solution.py:14
  150.4 34.2 %collective-permute-start.8 = (bf16[512,1024]{1,0:T(8,128)(2,1)S(1)}, bf16[512,1024]{1,0:T(8,128)(2,1)}, u32[]{:S(2)}, u32[]{:S(2)}) collective-permute-start(bf16[512,1024]{1,0:T(8,128)(2,1)S(1)} %collective-permute-done.6), channel_id=1, source_target_pairs={{0,2},{2,4},{4,6},{6,8},{8,10},{10,12},{12,14},{14,16},{16,18},{18... | collective-permute-start | bytes 3145736 | tf_op jit(solution)/shard_map/ppermute | solution.py:14
  152.3 32.3 %collective-permute-start.9 = (f32[512]{0:T(512)S(1)}, f32[512]{0:T(512)S(1)}, u32[]{:S(2)}, u32[]{:S(2)}) collective-permute-start(f32[512]{0:T(512)S(1)} %collective-permute-done.7), channel_id=1, source_target_pairs={{0,2},{2,4},{4,6},{6,8},{8,10},{10,12},{12,14},{14,16},{16,18},{18... | collective-permute-start | bytes 6152 | tf_op jit(solution)/shard_map/ppermute | solution.py:14
  186.4 0.7 copy-start.5
  187.5 41.8 %collective-permute-start.14 = (f32[512,1024]{1,0:T(8,128)S(1)}, f32[512,1024]{1,0:T(8,128)}, u32[]{:S(2)}, u32[]{:S(2)}) collective-permute-start(f32[512,1024]{1,0:T(8,128)S(1)} %add.199), channel_id=1, source_target_pairs={{0,2},{2,4},{4,6},{6,8},{8,10},{10,12},{12,14},{14,16},{16,18},{18... | collective-permute-start | bytes 6291464 | tf_op jit(solution)/shard_map/ppermute | solution.py:14
  192.0 34.3 %collective-permute-start.10 = (bf16[512,1024]{1,0:T(8,128)(2,1)}, bf16[512,1024]{1,0:T(8,128)(2,1)}, u32[]{:S(2)}, u32[]{:S(2)}) collective-permute-start(bf16[512,1024]{1,0:T(8,128)(2,1)} %collective-permute-done.8), channel_id=1, source_target_pairs={{0,2},{2,4},{4,6},{6,8},{8,10},{10,12},{12,14},{14,16},{16,18},{18... | collective-permute-start | bytes 3145736 | tf_op jit(solution)/shard_map/ppermute | solution.py:14
  193.9 32.4 %collective-permute-start.11 = (f32[512]{0:T(512)S(1)}, f32[512]{0:T(512)S(1)}, u32[]{:S(2)}, u32[]{:S(2)}) collective-permute-start(f32[512]{0:T(512)S(1)} %collective-permute-done.9), channel_id=1, source_target_pairs={{0,2},{2,4},{4,6},{6,8},{8,10},{10,12},{12,14},{14,16},{16,18},{18... | collective-permute-start | bytes 6152 | tf_op jit(solution)/shard_map/ppermute | solution.py:14
  228.2 0.7 copy-start.7
  232.6 1.2 copy-start.2
  232.6 1.7 copy-start.4
  234.4 1.0 copy-start.6
  235.4 1.7 copy-start.8
Sparse Core Ops, SparseCore 0:
  10.1 36.8 all-gather.3
  232.8 64.4 reduce-scatter.1
where the time goes:
time: 305 us; the launch traced here: 304 us
  waiting for transfers between devices  190 us (62%)
  starting transfers between devices  73.6 us (24%)
  between operations  15.1 us (5%)
  matrix products  15 us (5%)
  other arithmetic  4.85 us (2%)
  blocking collectives  3.19 us (1%)
    ppermute x15, waiting for transfers between devices, shifted(): return lax.ppermute(value, axis, pairs)  93.1 us
    ppermute x15, starting transfers between devices, shifted(): return lax.ppermute(value, axis, pairs)  73.5 us
    reduce_scatter x1, waiting for transfers between devices, local(): grad_text = lax.psum_scatter(accum, 'sub', scatter_dimension=0, tiled=True)  57.6 us
    all_gather x1, waiting for transfers between devices, local(): block = lax.all_gather(caption_vectors, 'sub', axis=0, tiled=True)  38.4 us
    dot_general x7, matrix products, inner(): lax.dot_general(left, right, (((1,), (1,)), ((), ())), preferred_element_...  7.75 us
  transfers between devices with their start and end apart: 17, of which 6 were waited for; matrix products, arithmetic and copies ran while one was open for 5% of the time, Pallas kernels for 0%

commit v1 on v0

v1 whole, which is shorter than its diff:
```python
import math

import jax
import jax.numpy as jnp
from jax import lax
from jax.experimental import pallas as pl
from jax.experimental.pallas import tpu as pltpu
from jax.sharding import PartitionSpec as P

MESH = pl.DeviceIdType.MESH
PARTS = 4
GPARTS = 2

R_SIB = 0
R_T0 = R_SIB + PARTS
R_T2 = R_T0 + 1
R_T3 = R_T2 + PARTS
R_P0 = R_T3 + 1
R_P1 = R_P0 + 1
R_STAT = R_P1 + PARTS
R_GSIB = R_STAT + 8
R_GT2 = R_GSIB + GPARTS
R_GT0 = R_GT2 + 1
R_GTX = R_GT0 + 1
R_GB = R_GTX + 1
N_SEM = R_GB + 2 * GPARTS

S_SIB, S_OTHER, S_NEXT, S_PREV, S_NEXT_X, S_PREV_X = 0, 1, 2, 4, 6, 7


def nt(a, b):
    return lax.dot_general(a, b, (((1,), (1,)), ((), ())), preferred_element_type=jnp.float32)


def tn(a, b):
    return lax.dot_general(a, b, (((0,), (0,)), ((), ())), preferred_element_type=jnp.float32)


def nn(a, b):
    return lax.dot_general(a, b, (((1,), (0,)), ((), ())), preferred_element_type=jnp.float32)


def lse_down(z):
    top = jnp.max(z, axis=0, keepdims=True)
    return top + jnp.log(jnp.sum(jnp.exp(z - top), axis=0, keepdims=True))


def lse_along(z):
    top = jnp.max(z, axis=1, keepdims=True)
    lse = top + jnp.log(jnp.sum(jnp.exp(z - top), axis=1, keepdims=True))
    return jnp.transpose(jnp.broadcast_to(lse, (z.shape[0], 128)))[0:1]


def joined(*parts):
    top = parts[0]
    for part in parts[1:]:
        top = jnp.maximum(top, part)
    total = jnp.exp(parts[0] - top)
    for part in parts[1:]:
        total = total + jnp.exp(part - top)
    return top + jnp.log(total)


def upright(row):
    return jnp.transpose(jnp.broadcast_to(row, (128, row.shape[1])))[:, 0:1]


def kernel(n_dp, heat, im, tx, pg, tg, iall, iprev, tall, z, w, stat, stats, stage, gsib, gt2, gt0, gtx, gb,
           send_sem, recv_sem):
    rows, depth = im.shape
    b = lax.axis_index("dp")
    s = lax.axis_index("sub")
    core = lax.rem(b, 2)
    chip = b // 2
    chips = n_dp // 2

    def level(c):
        return lax.rem(c // 4, 2)

    def at(step, k, flip):
        c = lax.rem(chip + (chips + step), chips)
        lane = lax.rem(s + level(chip) + level(c) + flip, 2)
        return (c * 2 + k, lane)

    scale = heat[0] * (1.0 / math.sqrt(depth))
    part = rows // PARTS
    gpart = rows // GPARTS
    own = slice(0, rows)
    sib = slice(rows, 2 * rows)

    def piece(p):
        return pl.ds(p * part, part)

    def gpiece(p):
        return pl.ds(p * gpart, gpart)

    def text(t):
        return pl.ds(t * rows, rows)

    def run(k):
        sent = []

        def send(src, dst, index, to):
            copy = pltpu.make_async_remote_copy(
                src_ref=src, dst_ref=dst, send_sem=send_sem.at[len(sent)], recv_sem=recv_sem.at[index],
                device_id=to, device_id_type=MESH)
            copy.start()
            sent.append(copy)

        def arrived(dst, index):
            pltpu.make_async_remote_copy(
                src_ref=dst, dst_ref=dst, send_sem=send_sem.at[0], recv_sem=recv_sem.at[index],
                device_id=sibling, device_id_type=MESH).wait_recv()

        sibling = at(0, k, 1)
        other = at(0, 1 - k, 0)
        partners = [sibling, other, at(1, 0, 0), at(1, 1, 0), at(-1, 0, 0), at(-1, 1, 0)]
        if k == 1:
            partners += [at(1, 1, 1), at(-1, 1, 1)]
        barrier = pltpu.get_barrier_semaphore()
        for partner in partners:
            pl.semaphore_signal(barrier, inc=1, device_id=partner, device_id_type=MESH)
        pl.semaphore_wait(barrier, len(partners))

        send(tx, tall.at[text(k)], R_T0, other)
        if k == 0:
            for p in range(PARTS):
                send(tx.at[piece(p)], tall.at[pl.ds(2 * rows + p * part, part)], R_T2 + p, at(-1, 0, 0))
            for p in range(PARTS):
                send(im.at[piece(p)], iall.at[pl.ds(rows + p * part, part)], R_SIB + p, sibling)
        else:
            for p in range(PARTS):
                send(im.at[piece(p)], iall.at[pl.ds(rows + p * part, part)], R_SIB + p, sibling)
            send(im, iprev.at[pl.ds(0, rows)], R_P0, at(1, 1, 0))
            send(tx, tall.at[text(3)], R_T3, at(-1, 0, 0))

        iall[own, :] = im[...]
        tall[text(k), :] = tx[...]

        def logits(images, half, t, column):
            z[half * rows:(half + 1) * rows, column * rows:(column + 1) * rows] = scale * nt(
                images[half * rows:(half + 1) * rows, :], tall[text(t), :])

        stat[...] = jnp.zeros_like(stat)
        if k == 0:
            logits(iall, 0, 0, 0)
            arrived(tall.at[text(1)], R_T0)
            logits(iall, 0, 1, 1)
            for p in range(PARTS):
                piece_ref = tall.at[pl.ds(2 * rows + p * part, part)]
                arrived(piece_ref, R_T2 + p)
                send(piece_ref, piece_ref, R_T2 + p, other)
            logits(iall, 0, 2, 2)
            for p in range(PARTS):
                arrived(iall.at[pl.ds(rows + p * part, part)], R_SIB + p)
            for t in range(3):
                logits(iall, 1, t, t)
                stat[t:t + 1, :] = lse_down(z[:, t * rows:(t + 1) * rows])
            arrived(tall.at[text(3)], R_T3)
            for half in range(2):
                logits(iall, half, 3, 3)
            stat[3:4, :] = lse_down(z[:, 3 * rows:])
            for half in range(2):
                stat[4 + half:5 + half, :] = lse_along(z[half * rows:(half + 1) * rows, :])
        else:
            logits(iall, 0, 1, 3)
            arrived(tall.at[text(0)], R_T0)
            for p in range(PARTS):
                piece_ref = iall.at[pl.ds(rows + p * part, part)]
                arrived(piece_ref, R_SIB + p)
                send(piece_ref, iprev.at[pl.ds(rows + p * part, part)], R_P1 + p, at(1, 1, 0))
            logits(iall, 1, 1, 3)
            for half in range(2):
                stat[4 + half:5 + half, :] = lse_along(z[half * rows:(half + 1) * rows, 3 * rows:])
            arrived(iprev.at[pl.ds(0, rows)], R_P0)
            logits(iprev, 0, 0, 0)
            logits(iprev, 0, 1, 1)
            for p in range(PARTS):
                arrived(tall.at[pl.ds(2 * rows + p * part, part)], R_T2 + p)
            logits(iprev, 0, 2, 2)
            stat[6:7, :] = lse_along(z[own, :3 * rows])
            for p in range(PARTS):
                arrived(iprev.at[pl.ds(rows + p * part, part)], R_P1 + p)
            for t in range(3):
                logits(iprev, 1, t, t)
            stat[7:8, :] = lse_along(z[sib, :3 * rows])
            stat[0:1, :] = lse_down(z[:, :rows])
            stat[1:2, :] = joined(lse_down(z[:, rows:2 * rows]), lse_down(z[:, 3 * rows:]))
            stat[2:3, :] = lse_down(z[:, 2 * rows:3 * rows])

        send(stat, stats.at[S_SIB], R_STAT + S_SIB, sibling)
        send(stat, stats.at[S_PREV + k], R_STAT + S_PREV + k, at(1, 0, 0))
        send(stat, stats.at[S_PREV + k], R_STAT + S_PREV + k, at(1, 1, 0))
        send(stat, stats.at[S_NEXT + k], R_STAT + S_NEXT + k, at(-1, 0, 0))
        send(stat, stats.at[S_NEXT + k], R_STAT + S_NEXT + k, at(-1, 1, 0))
        if k == 1:
            send(stat, stats.at[S_PREV_X], R_STAT + S_PREV_X, at(1, 1, 1))
            send(stat, stats.at[S_NEXT_X], R_STAT + S_NEXT_X, at(-1, 1, 1))
        send(stat, stats.at[S_OTHER], R_STAT + S_OTHER, other)
        for slot in range(6 if k == 0 else 8):
            arrived(stats.at[slot], R_STAT + slot)

        def line(slot, row):
            return stats[slot, row:row + 1, :]

        def mine(row):
            return stat[row:row + 1, :]

        col = [
            joined(mine(0), line(S_OTHER, 0), line(S_PREV, 2), line(S_PREV + 1, 2)),
            joined(mine(1), line(S_OTHER, 1), line(S_PREV, 3)),
            joined(mine(2), line(S_OTHER, 2), line(S_NEXT, 0), line(S_NEXT + 1, 0)),
        ]
        if k == 0:
            col.append(joined(mine(3), line(S_NEXT, 1), line(S_NEXT + 1, 1)))
            row_a = [upright(joined(mine(4 + h), line(S_SIB, 5 - h))) for h in range(2)]
        else:
            row_a = [
                upright(joined(mine(4 + h), line(S_SIB, 5 - h), line(S_NEXT + 1, 6 + h), line(S_NEXT_X, 7 - h)))
                for h in range(2)]
            row_b = [
                upright(joined(mine(6 + h), line(S_SIB, 7 - h), line(S_PREV + 1, 4 + h), line(S_PREV_X, 5 - h)))
                for h in range(2)]

        def weigh(half, column, row_lse, col_lse, diagonal):
            at_rows = slice(half * rows, (half + 1) * rows)
            at_cols = slice(column * rows, (column + 1) * rows)
            block = z[at_rows, at_cols]
            weight = jnp.exp(block - row_lse) + jnp.exp(block - col_lse)
            if diagonal:
                i = lax.broadcasted_iota(jnp.int32, (rows, rows), 0)
                j = lax.broadcasted_iota(jnp.int32, (rows, rows), 1)
                weight = weight - 2.0 * (i == j).astype(jnp.float32)
            w[at_rows, at_cols] = (0.5 * scale * weight).astype(jnp.bfloat16)

        def columns(column):
            return slice(column * rows, (column + 1) * rows)

        b16 = jnp.bfloat16
        f32 = jnp.float32
        if k == 0:
            for half in range(2):
                weigh(half, 3, row_a[half], col[3], False)
            stage[0] = tn(w[:, columns(3)], iall[...]).astype(b16)
            send(stage.at[0], gtx, R_GTX, at(1, 1, 0))
            for half in range(2):
                weigh(half, 2, row_a[half], col[2], False)
            part_2 = tn(w[:, columns(2)], iall[...])
            arrived(gt2, R_GT2)
            stage[1] = (part_2 + gt2[...].astype(f32)).astype(b16)
            send(stage.at[1], gtx, R_GTX, at(1, 0, 0))
            for t in range(2):
                weigh(1, t, row_a[1], col[t], False)
            stage[2] = nn(w[sib, :], tall[...]).astype(b16)
            for p in range(GPARTS):
                send(stage.at[2, gpiece(p)], gsib.at[gpiece(p)], R_GSIB + p, sibling)
            for t in range(2):
                weigh(0, t, row_a[0], col[t], t == 0)
            stage[3] = tn(w[:, columns(1)], iall[...]).astype(b16)
            send(stage.at[3], gt0, R_GT0, other)
            tg[...] = tn(w[:, columns(0)], iall[...])
            pg[...] = nn(w[own, :], tall[...])
            arrived(gt0, R_GT0)
            tg[...] += gt0[...].astype(f32)
            for p in range(GPARTS):
                arrived(gsib.at[gpiece(p)], R_GSIB + p)
                pg[gpiece(p), :] += gsib[gpiece(p), :].astype(f32)
            arrived(gtx, R_GTX)
            tg[...] += gtx[...].astype(f32)
        else:
            for half in range(2):
                weigh(half, 2, row_b[half], col[2], False)
            stage[0] = tn(w[:, columns(2)], iprev[...]).astype(b16)
            send(stage.at[0], gt2, R_GT2, other)
            for half in (1, 0):
                for t in range(2):
                    weigh(half, t, row_b[half], col[t], False)
                stage[1 + half] = nn(w[half * rows:(half + 1) * rows, :3 * rows], tall[pl.ds(0, 3 * rows), :]).astype(b16)
                for p in range(GPARTS):
                    send(stage.at[1 + half, gpiece(p)], gb.at[half, gpiece(p)], R_GB + half * GPARTS + p, at(-1, 1, 0))
            stage[3] = tn(w[:, columns(0)], iprev[...]).astype(b16)
            send(stage.at[3], gt0, R_GT0, other)
            for half in range(2):
                weigh(half, 3, row_a[half], col[1], half == 0)
            pg[...] = nn(w[sib, columns(3)], tall[text(1), :])
            tg[...] = tn(w[:, columns(1)], iprev[...]) + tn(w[:, columns(3)], iall[...])
            for p in range(GPARTS):
                arrived(gb.at[1, gpiece(p)], R_GB + GPARTS + p)
                stage[4, gpiece(p), :] = (pg[gpiece(p), :] + gb[1, gpiece(p), :].astype(f32)).astype(b16)
                send(stage.at[4, gpiece(p)], gsib.at[gpiece(p)], R_GSIB + p, sibling)
            pg[...] = nn(w[own, columns(3)], tall[text(1), :])
            arrived(gt0, R_GT0)
            tg[...] += gt0[...].astype(f32)
            arrived(gtx, R_GTX)
            tg[...] += gtx[...].astype(f32)
            for p in range(GPARTS):
                arrived(gb.at[0, gpiece(p)], R_GB + p)
                pg[gpiece(p), :] += gb[0, gpiece(p), :].astype(f32)
            for p in range(GPARTS):
                arrived(gsib.at[gpiece(p)], R_GSIB + p)
                pg[gpiece(p), :] += gsib[gpiece(p), :].astype(f32)
        for copy in sent:
            copy.wait_send()

    @pl.when(core == 0)
    def _():
        run(0)

    @pl.when(core == 1)
    def _():
        run(1)


def local(photo_vectors, caption_vectors, inverse_heat_factor):
    rows, depth = photo_vectors.shape
    n_dp = lax.axis_size("dp")
    vmem = pl.BlockSpec(memory_space=pltpu.VMEM)
    bf16 = jnp.bfloat16
    block = pltpu.VMEM((rows, depth), bf16)

    def body(*refs):
        kernel(n_dp, *refs)

    return pl.pallas_call(
        body,
        out_shape=[jax.ShapeDtypeStruct((rows, depth), jnp.float32)] * 2,
        in_specs=[pl.BlockSpec(memory_space=pltpu.SMEM), vmem, vmem],
        out_specs=[vmem, vmem],
        scratch_shapes=[
            pltpu.VMEM((2 * rows, depth), bf16),
            pltpu.VMEM((2 * rows, depth), bf16),
            pltpu.VMEM((4 * rows, depth), bf16),
            pltpu.VMEM((2 * rows, 4 * rows), jnp.float32),
            pltpu.VMEM((2 * rows, 4 * rows), bf16),
            pltpu.VMEM((8, rows), jnp.float32),
            pltpu.VMEM((8, 8, rows), jnp.float32),
            pltpu.VMEM((5, rows, depth), bf16),
            block,
            block,
            block,
            block,
            pltpu.VMEM((2, rows, depth), bf16),
            pltpu.SemaphoreType.DMA((40,)),
            pltpu.SemaphoreType.DMA((N_SEM,)),
        ],
        compiler_params=pltpu.CompilerParams(
            collective_id=0, has_side_effects=True, vmem_limit_bytes=48 * 2**20),
        cost_estimate=pl.CostEstimate(
            flops=6 * 2 * rows * 4 * rows * depth, bytes_accessed=12 * rows * depth,
            transcendentals=4 * 8 * rows * rows),
        name="banded",
    )(inverse_heat_factor, photo_vectors, caption_vectors)


def solution(mesh):
    in_specs = (P(("dp", "sub"), None), P(("dp", "sub"), None), P())
    out_specs = (P(("dp", "sub"), None), P(("dp", "sub"), None))
    return jax.shard_map(local, mesh=mesh, in_specs=in_specs, out_specs=out_specs, check_vma=False)
```

time: 305 us -> 62.2 us (0.20)
  waiting for transfers between devices: 190 us -> 0 us
  starting transfers between devices: 73.6 us -> 0 us
  Pallas kernels: 0 us -> 56.7 us
  matrix products: 15 us -> 0 us
  between operations: 15.1 us -> 1.29 us
  other arithmetic: 4.85 us -> 0 us
  blocking collectives: 3.19 us -> 0 us
    ppermute x15 -> x0, waiting for transfers between devices: 93.1 us -> none  [shifted(): return lax.ppermute(value, axis, pairs)]
    ppermute x15 -> x0, starting transfers between devices: 73.5 us -> none  [shifted(): return lax.ppermute(value, axis, pairs)]
    reduce_scatter x1 -> x0, waiting for transfers between devices: 57.6 us -> none  [local(): grad_text = lax.psum_scatter(accum, 'sub', scatter_dimension=0, tiled=True)]
    pallas_call x0 -> x1, Pallas kernels: none -> 56.7 us  [local(): pl.pallas_call(body, out_shape=[jax.ShapeDtypeStruct((rows, depth), jnp.f...]
    all_gather x1 -> x0, waiting for transfers between devices: 38.4 us -> none  [local(): block = lax.all_gather(caption_vectors, 'sub', axis=0, tiled=True)]
    dot_general x15 -> x0, matrix products: 15 us -> none  [the longest x7 7.75 us: inner(): lax.dot_general(left, right, (((1,), (1,)), ((), ())), preferred_element_...]
    add x7 -> x0, other arithmetic: 3.76 us -> none  [the longest x2 3.72 us: local(): accum = accum + across(weight, photo_vectors)]
    all_gather x1 -> x0, blocking collectives: 3.19 us -> none  [joined(): gathered = lax.all_gather(part, axis)]
  transfers between devices with their start and end apart: 17 -> 0, of which waited for: 6 -> 0; matrix products, arithmetic and copies ran while one was open for 5% -> 0% of each run, Pallas kernels for 0% -> 0%
where the time goes in v1:
time: 62.2 us; the launch traced here: 62 us
  Pallas kernels  56.7 us (91%)
  local copies, waits for them, and re-layouts  4.02 us (6%)
  between operations  1.29 us (2%)
    pallas_call x1, Pallas kernels, local(): pl.pallas_call(body, out_shape=[jax.ShapeDtypeStruct((rows, depth), jnp.f...  56.7 us
    unnamed x6, local copies, waits for them, and re-layouts  4.02 us

profile of v1, /device:TPU:1, one launch (start us, length us, event | category | flops | bytes accessed | tf_op | source)
XLA Modules:
  0.0 62.0 jit_solution(7797061496846579386)
XLA Ops:
  1.3 0.0 copy-start
  1.3 1.0 %copy-done = bf16[256,1024]{1,0:T(8,128)(2,1)S(1)} copy-done((bf16[256,1024]{1,0:T(8,128)(2,1)S(1)}, bf16[256,1024]{1,0:T(8,128)(2,1)}, u32[]{:S(2)}) %copy-start) | copy-done | bytes 524312
  2.3 0.0 copy-start.1
  2.3 1.0 %copy-done.1 = bf16[256,1024]{1,0:T(8,128)(2,1)S(1)} copy-done((bf16[256,1024]{1,0:T(8,128)(2,1)S(1)}, bf16[256,1024]{1,0:T(8,128)(2,1)}, u32[]{:S(2)}) %copy-start.1) | copy-done | bytes 524312
  3.4 56.7 %banded.1 = (f32[256,1024]{1,0:T(8,128)S(1)}, f32[256,1024]{1,0:T(8,128)S(1)}) custom-call(f32[1]{0:T(128)S(6)} %copy.7.refs_0_, bf16[256,1024]{1,0:T(8,128)(2,1)S(1)} %copy-done, bf16[256,1024]{1,0:T(8,128)(2,1)S(1)} %copy-done.1), custom_call_target="tpu_custom_call" | custom-call | flops 3221225472 | bytes 3145728 | tf_op jit(solution)/shard_map/banded/pallas_call | solution.py:324
  60.1 1.0 %copy.8 = f32[256,1024]{1,0:T(8,128)} copy(f32[256,1024]{1,0:T(8,128)S(1)} %get-tuple-element.4) | data formatting | bytes 2097152
  61.0 1.0 %copy.9 = f32[256,1024]{1,0:T(8,128)} copy(f32[256,1024]{1,0:T(8,128)S(1)} %get-tuple-element.5) | data formatting | bytes 2097152
Async XLA Ops:
  1.3 1.0 %copy-start = (bf16[256,1024]{1,0:T(8,128)(2,1)S(1)}, bf16[256,1024]{1,0:T(8,128)(2,1)}, u32[]{:S(2)}) copy-start(bf16[256,1024]{1,0:T(8,128)(2,1)} %refs_1_.1) | copy-start | bytes 1572868
  2.3 1.0 %copy-start.1 = (bf16[256,1024]{1,0:T(8,128)(2,1)S(1)}, bf16[256,1024]{1,0:T(8,128)(2,1)}, u32[]{:S(2)}) copy-start(bf16[256,1024]{1,0:T(8,128)(2,1)} %refs_2_.1) | copy-start | bytes 1572868

commit v2 on v1

--- a/solution.py
+++ b/solution.py
@@ -15,7 +15,7 @@
 R_T0 = R_SIB + PARTS
 R_T2 = R_T0 + 1
 R_T3 = R_T2 + PARTS
-R_P0 = R_T3 + 1
+R_P0 = R_T3 + PARTS
 R_P1 = R_P0 + 1
 R_STAT = R_P1 + PARTS
 R_GSIB = R_STAT + 8
@@ -65,8 +65,8 @@
     return jnp.transpose(jnp.broadcast_to(row, (128, row.shape[1])))[:, 0:1]
 
 
-def kernel(n_dp, heat, im, tx, pg, tg, iall, iprev, tall, z, w, stat, stats, stage, gsib, gt2, gt0, gtx, gb,
-           send_sem, recv_sem):
+def kernel(n_dp, heat, im, tx, pg, tg, gsib, gtx, iall, iprev, tall, z, w, stat, stats, stage, gt2, gt0, gb,
+           send_sem, recv_sem, load_sem):
     rows, depth = im.shape
     b = lax.axis_index("dp")
     s = lax.axis_index("sub")
@@ -99,6 +99,7 @@
 
     def run(k):
         sent = []
+        sent_early = []
 
         def send(src, dst, index, to):
             copy = pltpu.make_async_remote_copy(
@@ -115,87 +116,104 @@
         sibling = at(0, k, 1)
         other = at(0, 1 - k, 0)
         partners = [sibling, other, at(1, 0, 0), at(1, 1, 0), at(-1, 0, 0), at(-1, 1, 0)]
-        if k == 1:
-            partners += [at(1, 1, 1), at(-1, 1, 1)]
         barrier = pltpu.get_barrier_semaphore()
         for partner in partners:
             pl.semaphore_signal(barrier, inc=1, device_id=partner, device_id_type=MESH)
-        pl.semaphore_wait(barrier, len(partners))
-
-        send(tx, tall.at[text(k)], R_T0, other)
-        if k == 0:
-            for p in range(PARTS):
-                send(tx.at[piece(p)], tall.at[pl.ds(2 * rows + p * part, part)], R_T2 + p, at(-1, 0, 0))
-            for p in range(PARTS):
-                send(im.at[piece(p)], iall.at[pl.ds(rows + p * part, part)], R_SIB + p, sibling)
-        else:
-            for p in range(PARTS):
-                send(im.at[piece(p)], iall.at[pl.ds(rows + p * part, part)], R_SIB + p, sibling)
-            send(im, iprev.at[pl.ds(0, rows)], R_P0, at(1, 1, 0))
-            send(tx, tall.at[text(3)], R_T3, at(-1, 0, 0))
-
-        iall[own, :] = im[...]
-        tall[text(k), :] = tx[...]
+        load_text = pltpu.make_async_copy(tx, tall.at[text(k)], load_sem.at[0])
+        load_image = pltpu.make_async_copy(im, iall.at[pl.ds(0, rows)], load_sem.at[1])
+        load_text.start()
+        load_image.start()
 
         def logits(images, half, t, column):
             z[half * rows:(half + 1) * rows, column * rows:(column + 1) * rows] = scale * nt(
                 images[half * rows:(half + 1) * rows, :], tall[text(t), :])
 
+        def block(half, first, last):
+            return z[half * rows:(half + 1) * rows, first * rows:last * rows]
+
         stat[...] = jnp.zeros_like(stat)
+        load_text.wait()
+        load_image.wait()
+        logits(iall, 0, k, 0 if k == 0 else 3)
+        pl.semaphore_wait(barrier, len(partners))
+
+        def send_sib(p):
+            send(im.at[piece(p)], iall.at[pl.ds(rows + p * part, part)], R_SIB + p, sibling)
+
         if k == 0:
-            logits(iall, 0, 0, 0)
+            for p in range(PARTS):
+                send(tx.at[piece(p)], tall.at[pl.ds(2 * rows + p * part, part)], R_T2 + p, at(-1, 0, 0))
+            send(tx, tall.at[text(0)], R_T0, other)
+            send_sib(0)
             arrived(tall.at[text(1)], R_T0)
             logits(iall, 0, 1, 1)
             for p in range(PARTS):
                 piece_ref = tall.at[pl.ds(2 * rows + p * part, part)]
                 arrived(piece_ref, R_T2 + p)
                 send(piece_ref, piece_ref, R_T2 + p, other)
+                if p + 1 < PARTS:
+                    send_sib(p + 1)
             logits(iall, 0, 2, 2)
+            row_0 = lse_along(block(0, 0, 3))
             for p in range(PARTS):
                 arrived(iall.at[pl.ds(rows + p * part, part)], R_SIB + p)
             for t in range(3):
                 logits(iall, 1, t, t)
+            for t in range(3):
                 stat[t:t + 1, :] = lse_down(z[:, t * rows:(t + 1) * rows])
-            arrived(tall.at[text(3)], R_T3)
+            row_1 = lse_along(block(1, 0, 3))
+            for p in range(PARTS):
+                arrived(tall.at[pl.ds(3 * rows + p * part, part)], R_T3 + p)
             for half in range(2):
                 logits(iall, half, 3, 3)
             stat[3:4, :] = lse_down(z[:, 3 * rows:])
-            for half in range(2):
-                stat[4 + half:5 + half, :] = lse_along(z[half * rows:(half + 1) * rows, :])
+            stat[4:5, :] = joined(row_0, lse_along(block(0, 3, 4)))
+            stat[5:6, :] = joined(row_1, lse_along(block(1, 3, 4)))
         else:
-            logits(iall, 0, 1, 3)
-            arrived(tall.at[text(0)], R_T0)
+            def send_t3(p):
+                send(tx.at[piece(p)], tall.at[pl.ds(3 * rows + p * part, part)], R_T3 + p, at(-1, 0, 0))
+
+            for p in range(PARTS):
+                send_sib(p)
+            send(im, iprev.at[pl.ds(0, rows)], R_P0, at(1, 1, 0))
+            send(tx, tall.at[text(1)], R_T0, other)
+            send_t3(0)
             for p in range(PARTS):
                 piece_ref = iall.at[pl.ds(rows + p * part, part)]
                 arrived(piece_ref, R_SIB + p)
                 send(piece_ref, iprev.at[pl.ds(rows + p * part, part)], R_P1 + p, at(1, 1, 0))
+                if p + 1 < PARTS:
+                    send_t3(p + 1)
             logits(iall, 1, 1, 3)
             for half in range(2):
-                stat[4 + half:5 + half, :] = lse_along(z[half * rows:(half + 1) * rows, 3 * rows:])
+                stat[4 + half:5 + half, :] = lse_along(block(half, 3, 4))
+            col_a = lse_down(z[:, 3 * rows:])
+            arrived(tall.at[text(0)], R_T0)
             arrived(iprev.at[pl.ds(0, rows)], R_P0)
             logits(iprev, 0, 0, 0)
             logits(iprev, 0, 1, 1)
             for p in range(PARTS):
                 arrived(tall.at[pl.ds(2 * rows + p * part, part)], R_T2 + p)
             logits(iprev, 0, 2, 2)
-            stat[6:7, :] = lse_along(z[own, :3 * rows])
+            stat[6:7, :] = lse_along(block(0, 0, 3))
+            col_b = [lse_down(block(0, t, t + 1)) for t in range(3)]
+            col_b[1] = joined(col_b[1], col_a)
             for p in range(PARTS):
                 arrived(iprev.at[pl.ds(rows + p * part, part)], R_P1 + p)
             for t in range(3):
                 logits(iprev, 1, t, t)
-            stat[7:8, :] = lse_along(z[sib, :3 * rows])
-            stat[0:1, :] = lse_down(z[:, :rows])
-            stat[1:2, :] = joined(lse_down(z[:, rows:2 * rows]), lse_down(z[:, 3 * rows:]))
-            stat[2:3, :] = lse_down(z[:, 2 * rows:3 * rows])
-
-        send(stat, stats.at[S_SIB], R_STAT + S_SIB, sibling)
-        send(stat, stats.at[S_PREV + k], R_STAT + S_PREV + k, at(1, 0, 0))
-        send(stat, stats.at[S_PREV + k], R_STAT + S_PREV + k, at(1, 1, 0))
-        send(stat, stats.at[S_NEXT + k], R_STAT + S_NEXT + k, at(-1, 0, 0))
-        send(stat, stats.at[S_NEXT + k], R_STAT + S_NEXT + k, at(-1, 1, 0))
+            stat[7:8, :] = lse_along(block(1, 0, 3))
+            for t in range(3):
+                stat[t:t + 1, :] = joined(col_b[t], lse_down(block(1, t, t + 1)))
+
         if k == 1:
             send(stat, stats.at[S_PREV_X], R_STAT + S_PREV_X, at(1, 1, 1))
             send(stat, stats.at[S_NEXT_X], R_STAT + S_NEXT_X, at(-1, 1, 1))
+        send(stat, stats.at[S_PREV + k], R_STAT + S_PREV + k, at(1, 1, 0))
+        send(stat, stats.at[S_PREV + k], R_STAT + S_PREV + k, at(1, 0, 0))
+        send(stat, stats.at[S_NEXT + k], R_STAT + S_NEXT + k, at(-1, 1, 0))
+        send(stat, stats.at[S_NEXT + k], R_STAT + S_NEXT + k, at(-1, 0, 0))
+        send(stat, stats.at[S_SIB], R_STAT + S_SIB, sibling)
         send(stat, stats.at[S_OTHER], R_STAT + S_OTHER, other)
         for slot in range(6 if k == 0 else 8):
             arrived(stats.at[slot], R_STAT + slot)
@@ -243,17 +261,16 @@
                 weigh(half, 3, row_a[half], col[3], False)
             stage[0] = tn(w[:, columns(3)], iall[...]).astype(b16)
             send(stage.at[0], gtx, R_GTX, at(1, 1, 0))
-            for half in range(2):
-                weigh(half, 2, row_a[half], col[2], False)
+            for t in range(3):
+                weigh(1, t, row_a[1], col[t], False)
+            stage[2] = nn(w[sib, :], tall[...]).astype(b16)
+            for p in range(GPARTS):
+                send(stage.at[2, gpiece(p)], gsib.at[gpiece(p)], R_GSIB + p, sibling)
+            weigh(0, 2, row_a[0], col[2], False)
             part_2 = tn(w[:, columns(2)], iall[...])
             arrived(gt2, R_GT2)
             stage[1] = (part_2 + gt2[...].astype(f32)).astype(b16)
             send(stage.at[1], gtx, R_GTX, at(1, 0, 0))
-            for t in range(2):
-                weigh(1, t, row_a[1], col[t], False)
-            stage[2] = nn(w[sib, :], tall[...]).astype(b16)
-            for p in range(GPARTS):
-                send(stage.at[2, gpiece(p)], gsib.at[gpiece(p)], R_GSIB + p, sibling)
             for t in range(2):
                 weigh(0, t, row_a[0], col[t], t == 0)
             stage[3] = tn(w[:, columns(1)], iall[...]).astype(b16)
@@ -264,20 +281,20 @@
             tg[...] += gt0[...].astype(f32)
             for p in range(GPARTS):
                 arrived(gsib.at[gpiece(p)], R_GSIB + p)
-                pg[gpiece(p), :] += gsib[gpiece(p), :].astype(f32)
             arrived(gtx, R_GTX)
-            tg[...] += gtx[...].astype(f32)
         else:
-            for half in range(2):
-                weigh(half, 2, row_b[half], col[2], False)
+            for t in range(3):
+                weigh(1, t, row_b[1], col[t], False)
+            stage[2] = nn(w[sib, :3 * rows], tall[pl.ds(0, 3 * rows), :]).astype(b16)
+            first = len(sent)
+            for p in range(GPARTS):
+                send(stage.at[2, gpiece(p)], gb.at[1, gpiece(p)], R_GB + GPARTS + p, at(-1, 1, 0))
+            weigh(0, 2, row_b[0], col[2], False)
             stage[0] = tn(w[:, columns(2)], iprev[...]).astype(b16)
             send(stage.at[0], gt2, R_GT2, other)
-            for half in (1, 0):
-                for t in range(2):
-                    weigh(half, t, row_b[half], col[t], False)
-                stage[1 + half] = nn(w[half * rows:(half + 1) * rows, :3 * rows], tall[pl.ds(0, 3 * rows), :]).astype(b16)
-                for p in range(GPARTS):
-                    send(stage.at[1 + half, gpiece(p)], gb.at[half, gpiece(p)], R_GB + half * GPARTS + p, at(-1, 1, 0))
+            for t in range(2):
+                weigh(0, t, row_b[0], col[t], False)
+            stage[1] = nn(w[own, :3 * rows], tall[pl.ds(0, 3 * rows), :]).astype(b16)
             stage[3] = tn(w[:, columns(0)], iprev[...]).astype(b16)
             send(stage.at[3], gt0, R_GT0, other)
             for half in range(2):
@@ -285,22 +302,25 @@
             pg[...] = nn(w[sib, columns(3)], tall[text(1), :])
             tg[...] = tn(w[:, columns(1)], iprev[...]) + tn(w[:, columns(3)], iall[...])
             for p in range(GPARTS):
+                sent[first + p].wait_send()
+                send(stage.at[1, gpiece(p)], gb.at[0, gpiece(p)], R_GB + p, at(-1, 1, 0))
+            sent_early.extend(range(first, first + GPARTS))
+            for p in range(GPARTS):
                 arrived(gb.at[1, gpiece(p)], R_GB + GPARTS + p)
                 stage[4, gpiece(p), :] = (pg[gpiece(p), :] + gb[1, gpiece(p), :].astype(f32)).astype(b16)
                 send(stage.at[4, gpiece(p)], gsib.at[gpiece(p)], R_GSIB + p, sibling)
             pg[...] = nn(w[own, columns(3)], tall[text(1), :])
             arrived(gt0, R_GT0)
             tg[...] += gt0[...].astype(f32)
-            arrived(gtx, R_GTX)
-            tg[...] += gtx[...].astype(f32)
             for p in range(GPARTS):
                 arrived(gb.at[0, gpiece(p)], R_GB + p)
                 pg[gpiece(p), :] += gb[0, gpiece(p), :].astype(f32)
+            arrived(gtx, R_GTX)
             for p in range(GPARTS):
                 arrived(gsib.at[gpiece(p)], R_GSIB + p)
-                pg[gpiece(p), :] += gsib[gpiece(p), :].astype(f32)
-        for copy in sent:
-            copy.wait_send()
+        for index, copy in enumerate(sent):
+            if index not in sent_early:
+                copy.wait_send()
 
     @pl.when(core == 0)
     def _():
@@ -321,11 +341,13 @@
     def body(*refs):
         kernel(n_dp, *refs)
 
-    return pl.pallas_call(
+    hbm = pl.BlockSpec(memory_space=pltpu.HBM)
+    pg, tg, gsib, gtx = pl.pallas_call(
         body,
-        out_shape=[jax.ShapeDtypeStruct((rows, depth), jnp.float32)] * 2,
-        in_specs=[pl.BlockSpec(memory_space=pltpu.SMEM), vmem, vmem],
-        out_specs=[vmem, vmem],
+        out_shape=[jax.ShapeDtypeStruct((rows, depth), jnp.float32)] * 2
+        + [jax.ShapeDtypeStruct((rows, depth), bf16)] * 2,
+        in_specs=[pl.BlockSpec(memory_space=pltpu.SMEM), hbm, hbm],
+        out_specs=[vmem] * 4,
         scratch_shapes=[
             pltpu.VMEM((2 * rows, depth), bf16),
             pltpu.VMEM((2 * rows, depth), bf16),
@@ -337,11 +359,10 @@
             pltpu.VMEM((5, rows, depth), bf16),
             block,
             block,
-            block,
-            block,
             pltpu.VMEM((2, rows, depth), bf16),
             pltpu.SemaphoreType.DMA((40,)),
             pltpu.SemaphoreType.DMA((N_SEM,)),
+            pltpu.SemaphoreType.DMA((2,)),
         ],
         compiler_params=pltpu.CompilerParams(
             collective_id=0, has_side_effects=True, vmem_limit_bytes=48 * 2**20),
@@ -349,7 +370,8 @@
             flops=6 * 2 * rows * 4 * rows * depth, bytes_accessed=12 * rows * depth,
             transcendentals=4 * 8 * rows * rows),
         name="banded",
-    )(inverse_heat_factor, photo_vectors, caption_vectors)
+    )(inverse_heat_factor, pltpu.with_memory_space_constraint(photo_vectors, pltpu.HBM), pltpu.with_memory_space_constraint(caption_vectors, pltpu.HBM))
+    return pg + gsib.astype(jnp.float32), tg + gtx.astype(jnp.float32)
 
 
 def solution(mesh):

time: 62.2 us -> 58.6 us (0.942)
  local copies, waits for them, and re-layouts: 4.02 us -> 0 us
  other arithmetic: 0 us -> 1.77 us
  Pallas kernels: 56.7 us -> 55.4 us
    unnamed x6 -> x0, local copies, waits for them, and re-layouts: 4.02 us -> none
    add x0 -> x1, other arithmetic: none -> 1.77 us  [local(): return (pg + gsib.astype(jnp.float32), tg + gtx.astype(jnp.float32))]
    pallas_call x1, Pallas kernels: 56.7 us -> 55.4 us  [local(): pl.pallas_call(body, out_shape=[jax.ShapeDtypeStruct((rows, depth), jnp.f...]
where the time goes in v2:
time: 58.6 us; the launch traced here: 58.4 us
  Pallas kernels  55.4 us (95%)
  other arithmetic  1.77 us (3%)
  between operations  1.28 us (2%)
    pallas_call x1, Pallas kernels, local(): pl.pallas_call(body, out_shape=[jax.ShapeDtypeStruct((rows, depth), jnp.f...  55.4 us
    add x1, other arithmetic, local(): return (pg + gsib.astype(jnp.float32), tg + gtx.astype(jnp.float32))  1.77 us

profile of v2, /device:TPU:1, one launch (start us, length us, event | category | flops | bytes accessed | tf_op | source)
XLA Modules:
  0.0 58.4 jit_solution(1955580885401461949)
XLA Ops:
  1.3 55.4 %banded.1 = (f32[256,1024]{1,0:T(8,128)S(1)}, f32[256,1024]{1,0:T(8,128)S(1)}, bf16[256,1024]{1,0:T(8,128)(2,1)S(1)}, bf16[256,1024]{1,0:T(8,128)(2,1)S(1)}) custom-call(f32[1]{0:T(128)S(6)} %copy.5.refs_0_, bf16[256,1024]{1,0:T(8,128)(2,1)} %refs_1_.1, bf16[256,1024]{1,0:T(8,128)(2,1)} %refs_2_.1), custom_call_target="tpu_custom_call" | custom-call | flops 3221225472 | bytes 3145728 | tf_op jit(solution)/shard_map/banded/pallas_call | solution.py:345
  56.6 1.8 %convert_add_fusion = (f32[256,1024]{1,0:T(8,128)}, f32[256,1024]{1,0:T(8,128)}) fusion(f32[256,1024]{1,0:T(8,128)S(1)} %get-tuple-element.8, bf16[256,1024]{1,0:T(8,128)(2,1)S(1)} %get-tuple-element.9, f32[256,1024]{1,0:T(8,128)S(1)} %get-tuple-element.6, bf16[256,1024]{1,0:T(8,128)(2,1)S(1)} %get-tuple-element.7), kind=kLoop, calls=%fused_computation | loop fusion | flops 1048576 | bytes 5242880 | tf_op jit(solution)/shard_map/add | solution.py:374

commit v3 on v2

--- a/solution.py
+++ b/solution.py
@@ -77,10 +77,14 @@
     def level(c):
         return lax.rem(c // 4, 2)
 
+    near = {}
+    for step in (-1, 0, 1):
+        c = chip if step == 0 else lax.rem(chip + (chips + step), chips)
+        near[step] = (c * 2, s if step == 0 else lax.rem(s + level(chip) + level(c), 2))
+
     def at(step, k, flip):
-        c = lax.rem(chip + (chips + step), chips)
-        lane = lax.rem(s + level(chip) + level(c) + flip, 2)
-        return (c * 2 + k, lane)
+        first, lane = near[step]
+        return (first + k, 1 - lane if flip else lane)
 
     scale = heat[0] * (1.0 / math.sqrt(depth))
     part = rows // PARTS
@@ -144,15 +148,14 @@
             for p in range(PARTS):
                 send(tx.at[piece(p)], tall.at[pl.ds(2 * rows + p * part, part)], R_T2 + p, at(-1, 0, 0))
             send(tx, tall.at[text(0)], R_T0, other)
-            send_sib(0)
+            for p in range(PARTS):
+                send_sib(p)
             arrived(tall.at[text(1)], R_T0)
             logits(iall, 0, 1, 1)
             for p in range(PARTS):
                 piece_ref = tall.at[pl.ds(2 * rows + p * part, part)]
                 arrived(piece_ref, R_T2 + p)
                 send(piece_ref, piece_ref, R_T2 + p, other)
-                if p + 1 < PARTS:
-                    send_sib(p + 1)
             logits(iall, 0, 2, 2)
             row_0 = lse_along(block(0, 0, 3))
             for p in range(PARTS):
@@ -257,15 +260,14 @@
         b16 = jnp.bfloat16
         f32 = jnp.float32
         if k == 0:
-            for half in range(2):
-                weigh(half, 3, row_a[half], col[3], False)
+            for t in range(4):
+                weigh(1, t, row_a[1], col[t], False)
+            stage[2] = nn(w[sib, :], tall[...]).astype(b16)
+            for p in range(GPARTS):
+                send(stage.at[2, gpiece(p)], gsib.at[gpiece(p)], R_GSIB + p, sibling)
+            weigh(0, 3, row_a[0], col[3], False)
             stage[0] = tn(w[:, columns(3)], iall[...]).astype(b16)
             send(stage.at[0], gtx, R_GTX, at(1, 1, 0))
-            for t in range(3):
-                weigh(1, t, row_a[1], col[t], False)
-            stage[2] = nn(w[sib, :], tall[...]).astype(b16)
-            for p in range(GPARTS):
-                send(stage.at[2, gpiece(p)], gsib.at[gpiece(p)], R_GSIB + p, sibling)
             weigh(0, 2, row_a[0], col[2], False)
             part_2 = tn(w[:, columns(2)], iall[...])
             arrived(gt2, R_GT2)
@@ -301,11 +303,10 @@
                 weigh(half, 3, row_a[half], col[1], half == 0)
             pg[...] = nn(w[sib, columns(3)], tall[text(1), :])
             tg[...] = tn(w[:, columns(1)], iprev[...]) + tn(w[:, columns(3)], iall[...])
+            sent_early.extend(range(first, first + GPARTS))
             for p in range(GPARTS):
                 sent[first + p].wait_send()
                 send(stage.at[1, gpiece(p)], gb.at[0, gpiece(p)], R_GB + p, at(-1, 1, 0))
-            sent_early.extend(range(first, first + GPARTS))
-            for p in range(GPARTS):
                 arrived(gb.at[1, gpiece(p)], R_GB + GPARTS + p)
                 stage[4, gpiece(p), :] = (pg[gpiece(p), :] + gb[1, gpiece(p), :].astype(f32)).astype(b16)
                 send(stage.at[4, gpiece(p)], gsib.at[gpiece(p)], R_GSIB + p, sibling)
@@ -360,7 +361,7 @@
             block,
             block,
             pltpu.VMEM((2, rows, depth), bf16),
-            pltpu.SemaphoreType.DMA((40,)),
+            pltpu.SemaphoreType.DMA((64,)),
             pltpu.SemaphoreType.DMA((N_SEM,)),
             pltpu.SemaphoreType.DMA((2,)),
         ],

time: 58.6 us -> 57.3 us (0.978)
  Pallas kernels: 55.4 us -> 53.7 us
    pallas_call x1, Pallas kernels: 55.4 us -> 53.7 us  [local(): pl.pallas_call(body, out_shape=[jax.ShapeDtypeStruct((rows, depth), jnp.f...]
where the time goes in v3:
time: 57.3 us; the launch traced here: 56.7 us
  Pallas kernels  53.7 us (94%)
  other arithmetic  1.77 us (3%)
  between operations  1.28 us (2%)
    pallas_call x1, Pallas kernels, local(): pl.pallas_call(body, out_shape=[jax.ShapeDtypeStruct((rows, depth), jnp.f...  53.7 us
    add x1, other arithmetic, local(): return (pg + gsib.astype(jnp.float32), tg + gtx.astype(jnp.float32))  1.77 us

profile of v3, /device:TPU:1, one launch (start us, length us, event | category | flops | bytes accessed | tf_op | source)
XLA Modules:
  0.0 56.7 jit_solution(13060232933812845389)
XLA Ops:
  1.3 53.7 %banded.1 = (f32[256,1024]{1,0:T(8,128)S(1)}, f32[256,1024]{1,0:T(8,128)S(1)}, bf16[256,1024]{1,0:T(8,128)(2,1)S(1)}, bf16[256,1024]{1,0:T(8,128)(2,1)S(1)}) custom-call(f32[1]{0:T(128)S(6)} %copy.5.refs_0_, bf16[256,1024]{1,0:T(8,128)(2,1)} %refs_1_.1, bf16[256,1024]{1,0:T(8,128)(2,1)} %refs_2_.1), custom_call_target="tpu_custom_call" | custom-call | flops 3221225472 | bytes 3145728 | tf_op jit(solution)/shard_map/banded/pallas_call | solution.py:346
  55.0 1.8 %convert_add_fusion = (f32[256,1024]{1,0:T(8,128)}, f32[256,1024]{1,0:T(8,128)}) fusion(f32[256,1024]{1,0:T(8,128)S(1)} %get-tuple-element.8, bf16[256,1024]{1,0:T(8,128)(2,1)S(1)} %get-tuple-element.9, f32[256,1024]{1,0:T(8,128)S(1)} %get-tuple-element.6, bf16[256,1024]{1,0:T(8,128)(2,1)S(1)} %get-tuple-element.7), kind=kLoop, calls=%fused_computation | loop fusion | flops 1048576 | bytes 5242880 | tf_op jit(solution)/shard_map/add | solution.py:375
